TPU v7x, 256 devices: a whole 4x4x8 slice. The times are simulated.
256 devices in a mesh: tm: 4 (over x), orig: 64 (over z, y, core).
Axes of the slice: x: 4, y: 4, z: 8, core: 2. Of those that a mesh axis runs over, the one named last changes fastest.
Arguments:
- trip_counts: bfloat16 [12, 768, 256, 256], P('tm', 'orig'), may hold values from 0.25 to 4
- anchor_hour: float32 [12, 16384], P('tm', 'orig'), may hold values from 100 to 3000
- dest_hour: float32 [12, 32768], P('tm'), may hold values from 100 to 3000
- daily_target: bfloat16 [768, 256, 256], P('orig'), may hold values from 2 to 40
- block_columns: int32 [768], P('orig'), may hold values from -1 to 127, as said below
Outputs:
- fitted: bfloat16 [12, 768, 256, 256], P('tm', 'orig')
- dest_gap: float32 [12, 32768], P('tm', 'orig')
Inputs may be any that keep to these rules, and one draw needn't show every extreme that they name: `block_columns`: within each anchor block row the live column numbers are distinct and come first, followed by -1 for empty slots; every block row has at least one live slot, and some block row has all 12 live.
All inputs are finite; a program needn't handle non-finite values.
Results may differ from a plain program's by a relative error of at most 0.001.
Values sent between devices are 32-bit elements; how exact they have to be, the bound alone decides.
A program may use at most 64 MiB of HBM per device.

v0:
```python
import jax
import jax.numpy as jnp
from jax import lax
from jax.sharding import PartitionSpec as P


def cut_along(x, dim, length):
    dims = x.shape
    pieces = x.reshape(*dims[:dim], length, dims[dim] // length, *dims[dim + 1 :])
    return jnp.moveaxis(pieces, dim, 0)


def sum_at_owner(x, axis, dim):
    length = lax.axis_size(axis)
    pieces = lax.all_to_all(cut_along(x, dim, length), axis, 0, 0, tiled=True)
    return jnp.sum(pieces, axis=0)


def laid_out(pieces, dim):
    dims = list(pieces.shape[1:])
    dims[dim] *= pieces.shape[0]
    return jnp.moveaxis(pieces, 0, dim).reshape(dims)


def from_everyone(x, axis):
    copies = jnp.broadcast_to(x, (lax.axis_size(axis), *x.shape))
    return lax.all_to_all(copies, axis, split_axis=0, concat_axis=0, tiled=True)


def gather_directly(x, axis, dim):
    return laid_out(from_everyone(x, axis), dim)


def on_device(trip_counts, anchor_hour, dest_hour, daily_target, block_columns):
    bin_count = trip_counts.shape[0]
    block_side = trip_counts.shape[-1]
    column_blocks = dest_hour.shape[1] // block_side
    live_mask = (block_columns >= 0).astype(jnp.float32)
    onehot = (block_columns[:, None] == jnp.arange(column_blocks, dtype=jnp.int32)[None, :]).astype(
        jnp.float32
    )
    values = trip_counts.astype(jnp.float32) * live_mask[None, :, None, None]
    row_sums = jnp.sum(values, axis=(1, 3))
    anchor_fit = values * (anchor_hour / row_sums)[:, None, :, None]
    column_part = jnp.einsum(
        "tsj,sc->tcj", jnp.sum(anchor_fit, axis=2), onehot, precision=lax.Precision.HIGHEST
    )
    column_part = column_part.reshape(bin_count, column_blocks * block_side)
    shares = sum_at_owner(column_part, "orig", 1)
    span_width = shares.shape[1]
    offset = lax.axis_index("orig") * span_width
    target_span = lax.dynamic_slice_in_dim(dest_hour, offset, span_width, 1)
    dest_gain = gather_directly(target_span / jnp.maximum(shares, 1.0), "orig", 1)
    spread = jnp.einsum(
        "sc,tcj->tsj",
        onehot,
        dest_gain.reshape(bin_count, column_blocks, block_side),
        precision=lax.Precision.HIGHEST,
    )
    dest_fit = anchor_fit * spread[:, :, None, :]
    daily_part = jnp.sum(dest_fit, axis=0)
    daily_sum = lax.psum(daily_part, "tm")
    factor = daily_target.astype(jnp.float32) / (daily_sum + 1.0 - live_mask[:, None, None])
    daily_fit = dest_fit * factor[None]
    fitted = daily_fit.astype(jnp.bfloat16)
    final_part = jnp.einsum(
        "tsj,sc->tcj", jnp.sum(daily_fit, axis=2), onehot, precision=lax.Precision.HIGHEST
    )
    final_part = final_part.reshape(bin_count, column_blocks * block_side)
    final_share = sum_at_owner(final_part, "orig", 1)
    span_width = final_share.shape[1]
    offset = lax.axis_index("orig") * span_width
    target_span = lax.dynamic_slice_in_dim(dest_hour, offset, span_width, 1)
    dest_gap = final_share / target_span - 1.0
    return (fitted, dest_gap)


def solution(mesh):
    placed = (
        P("tm", "orig", None, None),
        P("tm", "orig"),
        P("tm", None),
        P("orig", None, None),
        P("orig"),
    )
    return jax.shard_map(
        on_device,
        mesh=mesh,
        in_specs=placed,
        out_specs=(P("tm", "orig", None, None), P("tm", "orig")),
        check_vma=False,
    )
```

profile of v0, /device:TPU:1, one launch (start us, length us, event | category | flops | bytes accessed | tf_op | source)
XLA Modules:
  0.0 200.2 jit_solution(14326123755778805820)
XLA Ops:
  7.2 0.8 compare_convert_fusion
  8.0 3.8 %fusion.1 = f32[3,256]{1,0:T(4,128)S(1)} fusion(bf16[3,12,256,256]{3,2,1,0:T(8,128)(2,1)} %param.5, f32[12]{0:T(128)S(1)} %compare_convert_fusion), kind=kLoop, calls=%fused_computation.2 | loop fusion | flops 7077120 | bytes 4721712 | tf_op jit(solution)/shard_map/reduce_sum | solution.py:43
  11.9 1.5 fusion.3
  13.4 0.4 convolution_bitcast_fusion.1
  13.9 0.1 reshape_reshape.9
  14.0 1.1 copy.13
  15.0 13.2 %all-to-all-start = ((f32[64,3,512]{2,1,0:T(4,128)}), f32[64,3,512]{2,1,0:T(4,128)S(1)}, u32[]{:S(2)}, u32[]{:S(2)}) async-start(f32[64,3,512]{2,1,0:T(4,128)} %bitcast.20), calls=%async_computation | async-start | bytes 1048576 | tf_op jit(solution)/shard_map/all_to_all | solution.py:15
  28.3 17.7 %all-to-all-done = f32[64,3,512]{2,1,0:T(4,128)S(1)} async-done(((f32[64,3,512]{2,1,0:T(4,128)}), f32[64,3,512]{2,1,0:T(4,128)S(1)}, u32[]{:S(2)}, u32[]{:S(2)}) %all-to-all-start) | async-done | bytes 393248 | tf_op jit(solution)/shard_map/all_to_all | solution.py:15
  45.9 0.1 reduce_sum.56
  46.0 0.7 maximum_divide_fusion
  46.7 0.1 broadcast_in_dim.2
  46.8 23.2 %all_to_all.15 = f32[64,3,512]{2,1,0:T(4,128)S(1)} all-to-all(f32[64,3,512]{2,1,0:T(4,128)S(1)} %broadcast_in_dim.2), channel_id=1, replica_groups=mesh['tm'=4,'orig'=64] {'orig'}, dimensions={0} | all-to-all | bytes 786432 | tf_op jit(solution)/shard_map/all_to_all | solution.py:27
  70.1 0.1 copy.8
  70.3 0.3 convolution_bitcast_fusion.2
  70.5 6.3 %fusion.5 = f32[12,256,256]{2,1,0:T(8,128)} fusion(bf16[3,12,256,256]{3,2,1,0:T(8,128)(2,1)} %param.5, f32[3,12,256]{2,1,0:T(8,128)S(1)} %convolution_bitcast_fusion.2, f32[3,256]{1,0:T(4,128)S(1)} %div.12, f32[12]{0:T(128)S(1)} %compare_convert_fusion), kind=kLoop, calls=%fused_computation.6 | loop fusion | flops 11010048 | bytes 7904304 | tf_op jit(solution)/shard_map/reduce_sum | solution.py:61
  76.8 77.4 %all-reduce.2.cloned.1.call-done = f32[12,256,256]{2,1,0:T(8,128)} async-done(((f32[12,256,256]{2,1,0:T(8,128)}), f32[12,256,256]{2,1,0:T(8,128)}) %all-reduce.2.cloned.1.call-update) | async-done | bytes 3145744 | tf_op jit(solution)/shard_map/psum | solution.py:62
  154.2 2.6 %subtract_divide_fusion = f32[12,256,256]{2,1,0:T(8,128)S(1)} fusion(f32[12,256,256]{2,1,0:T(8,128)} %all-reduce.2.cloned.1.call-done, bf16[12,256,256]{2,1,0:T(8,128)(2,1)S(1)} %copy-done.1, f32[12]{0:T(128)S(1)} %compare_convert_fusion), kind=kLoop, calls=%fused_computation.9 | loop fusion | flops 3145728 | bytes 7864368 | tf_op jit(solution)/shard_map/div | solution.py:63
  156.8 6.1 %fusion.6 = (f32[3,12,256]{2,1,0:T(8,128)S(1)}, bf16[3,12,256,256]{3,2,1,0:T(8,128)(2,1)}) fusion(bf16[3,12,256,256]{3,2,1,0:T(8,128)(2,1)} %param.5, f32[12,256,256]{2,1,0:T(8,128)S(1)} %subtract_divide_fusion, f32[3,12,256]{2,1,0:T(8,128)S(1)} %convolution_bitcast_fusion.2, f32[3,256]{1,0:T(4,128)S(1)} %div.12, f32[12]{0:T(128)S(1)} %compare_convert_fusion), kind=kLoop, calls=%fused_computation.7 | loop fusion | flops 16505856 | bytes 12659760 | tf_op jit(solution)/shard_map/reduce_sum | solution.py:67
  162.9 0.4 convolution_bitcast_fusion
  163.4 0.1 reshape_reshape.11
  163.5 0.3 copy.12
  163.8 28.2 %all_to_all.16 = f32[64,3,512]{2,1,0:T(4,128)S(1)} all-to-all(f32[64,3,512]{2,1,0:T(4,128)S(1)} %bitcast.22), channel_id=1, replica_groups=mesh['tm'=4,'orig'=64] {'orig'}, dimensions={0} | all-to-all | bytes 786432 | tf_op jit(solution)/shard_map/all_to_all | solution.py:15
  192.0 0.1 reduce_sum.59
  192.1 1.3 divide_add_fusion
  (12 shorter events, 0.1 us)
Async XLA Ops:
  7.2 4.7 %copy-start = (bf16[3,12,256,256]{3,2,1,0:T(8,128)(2,1)S(1)}, bf16[3,12,256,256]{3,2,1,0:T(8,128)(2,1)}, u32[]{:S(2)}) copy-start(bf16[3,12,256,256]{3,2,1,0:T(8,128)(2,1)} %param.5) | copy-start | bytes 14155780
  7.2 4.7 %copy-start.3 = (f32[3,256]{1,0:T(4,128)S(1)}, f32[3,256]{1,0:T(4,128)}, u32[]{:S(2)}) copy-start(f32[3,256]{1,0:T(4,128)} %param.6) | copy-start | bytes 9220
  8.0 5.4 %copy-start.2 = (s32[12]{0:T(128)S(1)}, s32[12]{0:T(128)}, u32[]{:S(2)}) copy-start(s32[12]{0:T(128)} %param.9) | copy-start | bytes 148
  15.0 30.9 %all-to-all-start = ((f32[64,3,512]{2,1,0:T(4,128)}), f32[64,3,512]{2,1,0:T(4,128)S(1)}, u32[]{:S(2)}, u32[]{:S(2)}) async-start(f32[64,3,512]{2,1,0:T(4,128)} %bitcast.20), calls=%async_computation | async-start | bytes 1048576 | tf_op jit(solution)/shard_map/all_to_all | solution.py:15
  28.2 126.0 %all-reduce.2.cloned.1.call-start = ((), (), s32[]{:S(2)}) async-start(), calls=%async_computation.3 | async-start | bytes 6291456 | tf_op jit(solution)/shard_map/psum | solution.py:62
  70.5 83.7 %copy-start.1 = (bf16[12,256,256]{2,1,0:T(8,128)(2,1)S(1)}, bf16[12,256,256]{2,1,0:T(8,128)(2,1)}, u32[]{:S(2)}) copy-start(bf16[12,256,256]{2,1,0:T(8,128)(2,1)} %param.8) | copy-start | bytes 4718596
Sparse Core Ops, SparseCore 0:
  77.0 77.1 all-reduce.1
where the time goes:
time: 201 us; the launch traced here: 200 us
  waiting for transfers between devices  95 us (47%)
  blocking collectives  51.4 us (26%)
  other arithmetic  23.4 us (12%)
  between operations  14.2 us (7%)
  starting transfers between devices  13.2 us (7%)
    psum x1, waiting for transfers between devices, on_device(): daily_sum = lax.psum(daily_part, 'tm')  77.4 us
    all_to_all x1, blocking collectives, sum_at_owner(): pieces = lax.all_to_all(cut_along(x, dim, length), axis, 0, 0, tiled=True)  28.2 us
    all_to_all x1, blocking collectives, from_everyone(): return lax.all_to_all(copies, axis, split_axis=0, concat_axis=0, tiled=True)  23.2 us
    all_to_all x1, waiting for transfers between devices, sum_at_owner(): pieces = lax.all_to_all(cut_along(x, dim, length), axis, 0, 0, tiled=True)  17.7 us
    all_to_all x1, starting transfers between devices, sum_at_owner(): pieces = lax.all_to_all(cut_along(x, dim, length), axis, 0, 0, tiled=True)  13.2 us
    reduce_sum x1, other arithmetic, on_device(): daily_part = jnp.sum(dest_fit, axis=0)  6.3 us
    reduce_sum x1, other arithmetic, on_device(): jnp.sum(daily_fit, axis=2)  6.14 us
  transfers between devices with their start and end apart: 2, of which 2 were waited for; matrix products, arithmetic and copies ran while one was open for 0% of the time, Pallas kernels for 0%

commit v1 on v0

v1 whole, which is shorter than its diff:
```python
import jax
import jax.numpy as jnp
from jax import lax
from jax.experimental import pallas as pl
from jax.experimental.pallas import tpu as pltpu
from jax.sharding import PartitionSpec as P

BINS = 3
SLOTS = 12
SIDE = 256
LANES = 128
GROUP = 8
DEPTH = 8
PIECE = DEPTH * BINS * 2
KEYS = 128
ROWS = 64
F32 = jnp.float32


def send(src, dst, send_sem, recv_sem, tm, orig):
    return pltpu.make_async_remote_copy(
        src_ref=src,
        dst_ref=dst,
        send_sem=send_sem,
        recv_sem=recv_sem,
        device_id=(tm, orig),
        device_id_type=pl.DeviceIdType.MESH,
    )


def kernel(
    cols_ref, keys_ref, anchor_ref, trips_ref, dest_ref, target_ref,
    fitted_ref, gap_ref,
    trips, part, factor, half_in, quarter_in, target, row_acc, anchor_fit, dest_row, dest8,
    onehot, sums, spread, gains, wide, wide_in, narrow, narrow_in, gain_z, gain_piece,
    wide2, wide2_in, narrow2, narrow2_in,
    trips_sem, target_sem, dest_sem, fitted_sem,
    half_s, half_r, quarter_s, quarter_r, back_s, back_r, whole_s, whole_r,
    wide_s, wide_r, narrow_s, narrow_r, gz_s, gz_r, gg_s, gg_r, wide2_s, wide2_r, narrow2_s, narrow2_r,
):
    x = lax.axis_index("tm")
    q = lax.axis_index("orig")
    z, g = q // GROUP, q % GROUP
    v = x // 2
    u = (x + v) % 2
    pa = x + 1 - 2 * (x % 2)
    pb = 3 - x
    group = [z * GROUP + (g + d) % GROUP for d in range(1, GROUP)]
    column = [((z + d) % DEPTH) * GROUP + g for d in range(1, DEPTH)]

    barrier = pltpu.get_barrier_semaphore()
    partners = [(x, o) for o in group + column] + [(pa, q), (pb, q)]
    for t_, o_ in partners:
        pl.semaphore_signal(barrier, inc=1, device_id=(t_, o_), device_id_type=pl.DeviceIdType.MESH)

    first, second = (pa, pb), (pb, pa)
    keep1, keep2 = (u, v), (v, u)
    kept64 = [pl.multiple_of(128 * h + 64 * keep1[h], 64) for h in range(2)]
    sent64 = [pl.multiple_of(128 * h + 64 * (1 - keep1[h]), 64) for h in range(2)]
    kept32 = [pl.multiple_of(kept64[h] + 32 * keep2[h], 32) for h in range(2)]
    sent32 = [pl.multiple_of(kept64[h] + 32 * (1 - keep2[h]), 32) for h in range(2)]

    def load_trips(s):
        return pltpu.make_async_copy(trips_ref.at[:, s], trips.at[s], trips_sem.at[s])

    def load_target(h):
        return pltpu.make_async_copy(
            target_ref.at[:, pl.ds(kept32[h], 32), :], target.at[h], target_sem.at[h]
        )

    load_dest = pltpu.make_async_copy(
        dest_ref.at[:, pl.ds(pl.multiple_of(q * 512, 512), 512)], dest_row, dest_sem
    )

    @pl.loop(0, SLOTS)
    def _(s):
        load_trips(s).start()

    load_dest.start()
    for h in range(2):
        load_target(h).start()

    r = lax.broadcasted_iota(jnp.int32, (GROUP * PIECE, KEYS), 0)
    rg = (r * 1366) >> 16
    rem = r - rg * 48
    rz = (rem * 10923) >> 16
    rem = rem - rz * 6
    row_key = (16 * rz + 2 * rg + (rem & 1)) * BINS + (rem >> 1)
    onehot[...] = jnp.where(row_key == keys_ref[...], 1.0, 0.0).astype(F32)

    diagonal = lax.broadcasted_iota(jnp.int32, (SIDE, SIDE), 0) == lax.broadcasted_iota(
        jnp.int32, (SIDE, SIDE), 1
    )
    row_acc[...] = jnp.zeros_like(row_acc)
    sums[...] = jnp.zeros_like(sums)
    narrow[...] = jnp.zeros_like(narrow)
    narrow2[...] = jnp.zeros_like(narrow2)
    dest8[...] = jnp.ones_like(dest8)

    @pl.loop(0, SLOTS)
    def _(s):
        load_trips(s).wait()
        live = jnp.where(cols_ref[s] >= 0, 1.0, 0.0).astype(F32)
        for t in range(BINS):
            for c in range(SIDE // ROWS):
                rows = pl.ds(c * ROWS, ROWS)
                left = trips[s, t, rows, pl.ds(0, LANES)].astype(F32)
                right = trips[s, t, rows, pl.ds(LANES, LANES)].astype(F32)
                row_acc[t, rows, :] += (left + right) * live

    for t in range(BINS):
        hour = jnp.sum(jnp.where(diagonal, anchor_ref[pl.ds(t, 1), :], 0.0), axis=1, keepdims=True)
        total = jnp.sum(row_acc[t], axis=1, keepdims=True)
        anchor_fit[t] = jnp.broadcast_to(hour / total, (SIDE, LANES))

    @pl.loop(0, SLOTS)
    def _(s):
        for t in range(BINS):
            for l in range(SIDE // LANES):
                lanes = pl.ds(l * LANES, LANES)
                acc = jnp.zeros((ROWS, LANES), F32)
                for c in range(SIDE // ROWS):
                    rows = pl.ds(c * ROWS, ROWS)
                    acc += trips[s, t, rows, lanes].astype(F32) * anchor_fit[t, rows, :]
                sums[s, pl.ds(t, 1), lanes] = jnp.sum(acc, axis=0, keepdims=True)

    pl.semaphore_wait(barrier, len(partners))

    def owner_sums(wide, wide_in, narrow, narrow_in, wide_s, wide_r, narrow_s, narrow_r):
        wide[...] = jnp.dot(
            onehot[...], sums[...].reshape(KEYS, SIDE), precision=lax.Precision.HIGHEST, preferred_element_type=F32
        )
        copies = []
        for d in range(1, GROUP):
            other = pl.multiple_of(((g + d) % GROUP) * PIECE, PIECE)
            copies.append(
                send(wide.at[pl.ds(other, PIECE), :], wide_in.at[d - 1], wide_s.at[d - 1], wide_r.at[d - 1], x, group[d - 1])
            )
            copies[-1].start()
        total = wide[pl.ds(pl.multiple_of(g * PIECE, PIECE), PIECE), :]
        for d in range(1, GROUP):
            copies[d - 1].wait_recv()
            total = total + wide_in[d - 1]
        for c in range(DEPTH):
            narrow[c, pl.ds(0, 6), :] = total[6 * c : 6 * c + 6, :]
        more = []
        for d in range(1, DEPTH):
            more.append(
                send(narrow.at[(z + d) % DEPTH], narrow_in.at[d - 1], narrow_s.at[d - 1], narrow_r.at[d - 1], x, column[d - 1])
            )
            more[-1].start()
        total = narrow[z]
        for d in range(1, DEPTH):
            more[d - 1].wait_recv()
            total = total + narrow_in[d - 1]
        return total, copies + more

    load_dest.wait()
    for t in range(BINS):
        for b in range(2):
            dest8[pl.ds(2 * t + b, 1), :] = dest_row[pl.ds(t, 1), pl.ds(b * SIDE, SIDE)]

    total, pending = owner_sums(wide, wide_in, narrow, narrow_in, wide_s, wide_r, narrow_s, narrow_r)
    gain_z[z] = dest8[...] / jnp.maximum(total, 1.0)
    copies = []
    for d in range(1, DEPTH):
        copies.append(send(gain_z.at[z], gain_z.at[z], gz_s.at[d - 1], gz_r.at[d - 1], x, column[d - 1]))
        copies[-1].start()
    for copy in copies:
        copy.wait_recv()
    pending += copies
    for c in range(DEPTH):
        gain_piece[pl.ds(6 * c, 6), :] = gain_z[c, pl.ds(0, 6), :]
    mine = pl.ds(pl.multiple_of(g * PIECE, PIECE), PIECE)
    copies = []
    for d in range(1, GROUP):
        copies.append(send(gain_piece, gains.at[mine, :], gg_s.at[d - 1], gg_r.at[d - 1], x, group[d - 1]))
        copies[-1].start()
    gains[mine, :] = gain_piece[...]
    for copy in copies:
        copy.wait_recv()
    pending += copies
    spread[...] = lax.dot_general(
        onehot[...], gains[...], (((0,), (0,)), ((), ())),
        precision=lax.Precision.HIGHEST, preferred_element_type=F32,
    ).reshape(KEYS // 8, 8, SIDE)
    for h in range(2):
        load_target(h).wait()

    def halves(s, h):
        return send(
            part.at[s, pl.ds(sent64[h], 64), :], half_in.at[s, h], half_s.at[s, h], half_r.at[s, h], first[h], q
        )

    def quarters(s, h):
        return send(
            part.at[s, pl.ds(sent32[h], 32), :], quarter_in.at[s, h], quarter_s.at[s, h], quarter_r.at[s, h], second[h], q
        )

    def back(s, h):
        rows = pl.ds(kept32[h], 32)
        return send(factor.at[s, rows, :], factor.at[s, rows, :], back_s.at[s, h], back_r.at[s, h], second[h], q)

    def whole(s, h):
        rows = pl.ds(kept64[h], 64)
        return send(factor.at[s, rows, :], factor.at[s, rows, :], whole_s.at[s, h], whole_r.at[s, h], first[h], q)

    def store_fitted(s):
        return pltpu.make_async_copy(trips.at[s], fitted_ref.at[:, s], fitted_sem.at[s])

    @pl.loop(0, SLOTS + 4)
    def _(k):
        @pl.when(k < SLOTS)
        def _():
            s = k
            for l in range(SIDE // LANES):
                lanes = pl.ds(l * LANES, LANES)
                gain = [spread[s, pl.ds(t, 1), lanes] for t in range(BINS)]
                for c in range(SIDE // ROWS):
                    rows = pl.ds(c * ROWS, ROWS)
                    acc = jnp.zeros((ROWS, LANES), F32)
                    for t in range(BINS):
                        acc += trips[s, t, rows, lanes].astype(F32) * anchor_fit[t, rows, :] * gain[t]
                    part[s, rows, lanes] = acc
            for h in range(2):
                halves(s, h).start()

        @pl.when((k >= 1) & (k < SLOTS + 1))
        def _():
            s = k - 1
            for h in range(2):
                halves(s, h).wait_recv()
                part[s, pl.ds(kept64[h], 64), :] += half_in[s, h]
                quarters(s, h).start()

        @pl.when((k >= 2) & (k < SLOTS + 2))
        def _():
            s = k - 2
            dead = jnp.where(cols_ref[s] >= 0, 0.0, 1.0).astype(F32)
            for h in range(2):
                quarters(s, h).wait_recv()
                rows = pl.ds(kept32[h], 32)
                daily = part[s, rows, :] + quarter_in[s, h]
                factor[s, rows, :] = target[h, s].astype(F32) / (daily + dead)
                back(s, h).start()

        @pl.when((k >= 3) & (k < SLOTS + 3))
        def _():
            s = k - 3
            for h in range(2):
                back(s, h).wait_recv()
                whole(s, h).start()

        @pl.when(k >= 4)
        def _():
            s = k - 4
            for h in range(2):
                whole(s, h).wait_recv()
            for t in range(BINS):
                for l in range(SIDE // LANES):
                    lanes = pl.ds(l * LANES, LANES)
                    gain = spread[s, pl.ds(t, 1), lanes]
                    acc = jnp.zeros((ROWS, LANES), F32)
                    for c in range(SIDE // ROWS):
                        rows = pl.ds(c * ROWS, ROWS)
                        value = trips[s, t, rows, lanes].astype(F32) * anchor_fit[t, rows, :] * factor[s, rows, lanes]
                        acc += value
                        trips[s, t, rows, lanes] = (value * gain).astype(jnp.bfloat16)
                    sums[s, pl.ds(t, 1), lanes] = jnp.sum(acc, axis=0, keepdims=True) * gain
            store_fitted(s).start()

    total, more = owner_sums(wide2, wide2_in, narrow2, narrow2_in, wide2_s, wide2_r, narrow2_s, narrow2_r)
    pending += more
    gap = total / dest8[...] - 1.0
    for t in range(BINS):
        for b in range(2):
            gap_ref[pl.ds(t, 1), pl.ds(b * SIDE, SIDE)] = gap[2 * t + b : 2 * t + b + 1, :]

    for copy in pending:
        copy.wait_send()

    @pl.loop(0, SLOTS)
    def _(s):
        for h in range(2):
            halves(s, h).wait_send()
            quarters(s, h).wait_send()
            back(s, h).wait_send()
            whole(s, h).wait_send()
        store_fitted(s).wait()


def on_device(trip_counts, anchor_hour, dest_hour, daily_target, block_columns):
    bins = jnp.arange(8, dtype=jnp.int32)[None, :]
    keys = jnp.where(
        (block_columns[:, None] >= 0) & (bins < BINS), block_columns[:, None] * BINS + bins, -1
    ).reshape(1, SLOTS * 8)
    keys = jnp.pad(keys, ((0, 0), (0, KEYS - SLOTS * 8)), constant_values=-1)
    vmem = lambda *shape: pltpu.VMEM(shape, F32)
    dma = lambda *shape: pltpu.SemaphoreType.DMA(shape)
    scratch = [
        pltpu.VMEM((SLOTS, BINS, SIDE, SIDE), jnp.bfloat16),
        vmem(SLOTS, SIDE, SIDE),
        vmem(SLOTS, SIDE, SIDE),
        vmem(SLOTS, 2, 64, SIDE),
        vmem(SLOTS, 2, 32, SIDE),
        pltpu.VMEM((2, SLOTS, 32, SIDE), jnp.bfloat16),
        vmem(BINS, SIDE, LANES),
        vmem(BINS, SIDE, LANES),
        vmem(BINS, 512),
        vmem(8, SIDE),
        vmem(GROUP * PIECE, KEYS),
        vmem(KEYS // 8, 8, SIDE),
        vmem(KEYS // 8, 8, SIDE),
        vmem(GROUP * PIECE, SIDE),
        vmem(GROUP * PIECE, SIDE),
        vmem(GROUP - 1, PIECE, SIDE),
        vmem(DEPTH, 8, SIDE),
        vmem(DEPTH - 1, 8, SIDE),
        vmem(DEPTH, 8, SIDE),
        vmem(PIECE, SIDE),
        vmem(GROUP * PIECE, SIDE),
        vmem(GROUP - 1, PIECE, SIDE),
        vmem(DEPTH, 8, SIDE),
        vmem(DEPTH - 1, 8, SIDE),
        dma(SLOTS), dma(2), pltpu.SemaphoreType.DMA, dma(SLOTS),
    ] + [dma(SLOTS, 2)] * 8 + [dma(7)] * 12
    fitted, gap = pl.pallas_call(
        kernel,
        out_shape=(
            jax.ShapeDtypeStruct(trip_counts.shape, jnp.bfloat16),
            jax.ShapeDtypeStruct((BINS, 512), F32),
        ),
        in_specs=[
            pl.BlockSpec(memory_space=pltpu.SMEM),
            pl.BlockSpec(memory_space=pltpu.VMEM),
            pl.BlockSpec(memory_space=pltpu.VMEM),
            pl.BlockSpec(memory_space=pl.ANY),
            pl.BlockSpec(memory_space=pl.ANY),
            pl.BlockSpec(memory_space=pl.ANY),
        ],
        out_specs=(pl.BlockSpec(memory_space=pl.ANY), pl.BlockSpec(memory_space=pltpu.VMEM)),
        scratch_shapes=scratch,
        compiler_params=pltpu.CompilerParams(
            collective_id=0, has_side_effects=True, vmem_limit_bytes=40 * 1024 * 1024
        ),
        cost_estimate=pl.CostEstimate(flops=40_000_000, bytes_accessed=11_000_000, transcendentals=0),
    )(block_columns, keys, anchor_hour, trip_counts, dest_hour, daily_target)
    return fitted, gap


def solution(mesh):
    placed = (
        P("tm", "orig", None, None),
        P("tm", "orig"),
        P("tm", None),
        P("orig", None, None),
        P("orig"),
    )
    return jax.shard_map(
        on_device,
        mesh=mesh,
        in_specs=placed,
        out_specs=(P("tm", "orig", None, None), P("tm", "orig")),
        check_vma=False,
    )
```

time: 201 us -> 116 us (0.58)
  Pallas kernels: 0 us -> 105 us
  waiting for transfers between devices: 95 us -> 0 us
  blocking collectives: 51.4 us -> 0 us
  other arithmetic: 23.4 us -> 1.4 us
  between operations: 14.2 us -> 0.66 us
  starting transfers between devices: 13.2 us -> 0 us
  local copies, waits for them, and re-layouts: 1.84 us -> 9 us
    pallas_call x0 -> x1, Pallas kernels: none -> 105 us  [on_device(): pl.pallas_call(kernel, out_shape=(jax.ShapeDtypeStruct(trip_counts.shape,...]
    psum x1 -> x0, waiting for transfers between devices: 77.4 us -> none  [on_device(): daily_sum = lax.psum(daily_part, 'tm')]
    all_to_all x2 -> x0, blocking collectives: 51.4 us -> none  [the longest x1 28.2 us: sum_at_owner(): pieces = lax.all_to_all(cut_along(x, dim, length), axis, 0, 0, tiled=True)]
    reduce_sum x6 -> x0, other arithmetic: 18 us -> none  [the longest x1 6.3 us: on_device(): daily_part = jnp.sum(dest_fit, axis=0)]
    all_to_all x1 -> x0, waiting for transfers between devices: 17.7 us -> none  [sum_at_owner(): pieces = lax.all_to_all(cut_along(x, dim, length), axis, 0, 0, tiled=True)]
    all_to_all x1 -> x0, starting transfers between devices: 13.2 us -> none  [sum_at_owner(): pieces = lax.all_to_all(cut_along(x, dim, length), axis, 0, 0, tiled=True)]
    unnamed x8 -> x12, local copies, waits for them, and re-layouts: 0.02 us -> 8.91 us
    div x3 -> x0, other arithmetic: 3.27 us -> none  [the longest x1 2.56 us: on_device(): daily_target.astype(jnp.float32)]
  transfers between devices with their start and end apart: 2 -> 0, of which waited for: 2 -> 0; matrix products, arithmetic and copies ran while one was open for 0% -> 0% of each run, Pallas kernels for 0% -> 0%
where the time goes in v1:
time: 116 us
  Pallas kernels  105 us (91%)
  local copies, waits for them, and re-layouts  9 us (8%)
  other arithmetic  1.4 us (1%)
    pallas_call x1, Pallas kernels, on_device(): pl.pallas_call(kernel, out_shape=(jax.ShapeDtypeStruct(trip_counts.shape,...  105 us
    unnamed x12, local copies, waits for them, and re-layouts  8.91 us

profile of v1, /device:TPU:1, one launch (start us, length us, event | category | flops | bytes accessed | tf_op | source)
XLA Modules:
  0.0 115.9 jit_solution(12358485150270961072)
XLA Ops:
  0.6 0.7 broadcast_compare_fusion
  1.3 0.7 broadcast_multiply_fusion
  2.0 0.1 add_select_fusion
  2.0 0.1 select_n.15
  2.1 0.0 copy-start
  2.1 2.3 %copy-done = bf16[3,12,256,256]{3,2,1,0:T(8,128)(2,1)S(1)} copy-done((bf16[3,12,256,256]{3,2,1,0:T(8,128)(2,1)S(1)}, bf16[3,12,256,256]{3,2,1,0:T(8,128)(2,1)}, u32[]{:S(2)}) %copy-start) | copy-done | bytes 4718616
  4.5 0.0 copy-start.1
  4.5 1.4 %copy-done.1 = bf16[12,256,256]{2,1,0:T(8,128)(2,1)S(1)} copy-done((bf16[12,256,256]{2,1,0:T(8,128)(2,1)S(1)}, bf16[12,256,256]{2,1,0:T(8,128)(2,1)}, u32[]{:S(2)}) %copy-start.1) | copy-done | bytes 1572888
  5.9 0.0 copy-start.2
  5.9 1.0 copy-done.2
  6.9 0.0 copy-start.3
  6.9 0.7 copy-done.3
  7.6 0.0 copy-start.4
  7.6 0.7 copy-done.4
  8.3 104.8 %shard_map.68 = (bf16[3,12,256,256]{3,2,1,0:T(8,128)(2,1)S(1)}, f32[3,512]{1,0:T(4,128)S(1)}) custom-call(s32[12]{0:T(128)S(1)} %copy-done.4, s32[1,128]{1,0:T(1,128)S(1)} %pad.4.keys_ref, f32[3,256]{1,0:T(4,128)S(1)} %copy-done.3, bf16[3,12,256,256]{3,2,1,0:T(8,128)(2,1)S(1)} %copy-done, f32[3,32768]{1,0:T(4,128)S(1)} %copy-done.2, ...), custom_call_target="tpu_custom_call" | custom-call | flops 40000000 | bytes 11000000 | tf_op jit(solution)/shard_map/pallas_call | solution.py:327
  113.1 2.2 %copy.9 = bf16[3,12,256,256]{3,2,1,0:T(8,128)(2,1)} copy(bf16[3,12,256,256]{3,2,1,0:T(8,128)(2,1)S(1)} %get-tuple-element.4) | data formatting | bytes 9437184
  115.3 0.6 copy.10
  (2 shorter events, 0.0 us)
Async XLA Ops:
  2.1 2.3 %copy-start = (bf16[3,12,256,256]{3,2,1,0:T(8,128)(2,1)S(1)}, bf16[3,12,256,256]{3,2,1,0:T(8,128)(2,1)}, u32[]{:S(2)}) copy-start(bf16[3,12,256,256]{3,2,1,0:T(8,128)(2,1)} %trips_ref.1) | copy-start | bytes 14155780
  4.5 1.4 %copy-start.1 = (bf16[12,256,256]{2,1,0:T(8,128)(2,1)S(1)}, bf16[12,256,256]{2,1,0:T(8,128)(2,1)}, u32[]{:S(2)}) copy-start(bf16[12,256,256]{2,1,0:T(8,128)(2,1)} %target_ref.1) | copy-start | bytes 4718596
  5.9 1.0 copy-start.2
  6.9 0.7 copy-start.3
  7.6 0.7 copy-start.4

commit v2 on v1

--- a/solution.py
+++ b/solution.py
@@ -14,6 +14,7 @@
 PIECE = DEPTH * BINS * 2
 KEYS = 128
 ROWS = 64
+LAG = 2
 F32 = jnp.float32
 
 
@@ -29,7 +30,7 @@
 
 
 def kernel(
-    cols_ref, keys_ref, anchor_ref, trips_ref, dest_ref, target_ref,
+    cols_ref, anchor_ref, trips_ref, dest_ref, target_ref,
     fitted_ref, gap_ref,
     trips, part, factor, half_in, quarter_in, target, row_acc, anchor_fit, dest_row, dest8,
     onehot, sums, spread, gains, wide, wide_in, narrow, narrow_in, gain_z, gain_piece,
@@ -86,7 +87,13 @@
     rz = (rem * 10923) >> 16
     rem = rem - rz * 6
     row_key = (16 * rz + 2 * rg + (rem & 1)) * BINS + (rem >> 1)
-    onehot[...] = jnp.where(row_key == keys_ref[...], 1.0, 0.0).astype(F32)
+    lane = lax.broadcasted_iota(jnp.int32, (1, KEYS), 1)
+    key = jnp.full((1, KEYS), -1, jnp.int32)
+    for s in range(SLOTS):
+        col = cols_ref[s]
+        in_slot = (lane >= 8 * s) & (lane < 8 * s + BINS) & (jnp.full((1, KEYS), col, jnp.int32) >= 0)
+        key = jnp.where(in_slot, col * BINS + lane - 8 * s, key)
+    onehot[...] = jnp.where(row_key == key, 1.0, 0.0).astype(F32)
 
     diagonal = lax.broadcasted_iota(jnp.int32, (SIDE, SIDE), 0) == lax.broadcasted_iota(
         jnp.int32, (SIDE, SIDE), 1
@@ -208,7 +215,7 @@
     def store_fitted(s):
         return pltpu.make_async_copy(trips.at[s], fitted_ref.at[:, s], fitted_sem.at[s])
 
-    @pl.loop(0, SLOTS + 4)
+    @pl.loop(0, SLOTS + 4 * LAG)
     def _(k):
         @pl.when(k < SLOTS)
         def _():
@@ -225,17 +232,17 @@
             for h in range(2):
                 halves(s, h).start()
 
-        @pl.when((k >= 1) & (k < SLOTS + 1))
-        def _():
-            s = k - 1
+        @pl.when((k >= LAG) & (k < SLOTS + LAG))
+        def _():
+            s = k - LAG
             for h in range(2):
                 halves(s, h).wait_recv()
                 part[s, pl.ds(kept64[h], 64), :] += half_in[s, h]
                 quarters(s, h).start()
 
-        @pl.when((k >= 2) & (k < SLOTS + 2))
-        def _():
-            s = k - 2
+        @pl.when((k >= 2 * LAG) & (k < SLOTS + 2 * LAG))
+        def _():
+            s = k - 2 * LAG
             dead = jnp.where(cols_ref[s] >= 0, 0.0, 1.0).astype(F32)
             for h in range(2):
                 quarters(s, h).wait_recv()
@@ -244,16 +251,16 @@
                 factor[s, rows, :] = target[h, s].astype(F32) / (daily + dead)
                 back(s, h).start()
 
-        @pl.when((k >= 3) & (k < SLOTS + 3))
-        def _():
-            s = k - 3
+        @pl.when((k >= 3 * LAG) & (k < SLOTS + 3 * LAG))
+        def _():
+            s = k - 3 * LAG
             for h in range(2):
                 back(s, h).wait_recv()
                 whole(s, h).start()
 
-        @pl.when(k >= 4)
-        def _():
-            s = k - 4
+        @pl.when(k >= 4 * LAG)
+        def _():
+            s = k - 4 * LAG
             for h in range(2):
                 whole(s, h).wait_recv()
             for t in range(BINS):
@@ -290,11 +297,6 @@
 
 
 def on_device(trip_counts, anchor_hour, dest_hour, daily_target, block_columns):
-    bins = jnp.arange(8, dtype=jnp.int32)[None, :]
-    keys = jnp.where(
-        (block_columns[:, None] >= 0) & (bins < BINS), block_columns[:, None] * BINS + bins, -1
-    ).reshape(1, SLOTS * 8)
-    keys = jnp.pad(keys, ((0, 0), (0, KEYS - SLOTS * 8)), constant_values=-1)
     vmem = lambda *shape: pltpu.VMEM(shape, F32)
     dma = lambda *shape: pltpu.SemaphoreType.DMA(shape)
     scratch = [
@@ -333,7 +335,6 @@
         in_specs=[
             pl.BlockSpec(memory_space=pltpu.SMEM),
             pl.BlockSpec(memory_space=pltpu.VMEM),
-            pl.BlockSpec(memory_space=pltpu.VMEM),
             pl.BlockSpec(memory_space=pl.ANY),
             pl.BlockSpec(memory_space=pl.ANY),
             pl.BlockSpec(memory_space=pl.ANY),
@@ -344,7 +345,7 @@
             collective_id=0, has_side_effects=True, vmem_limit_bytes=40 * 1024 * 1024
         ),
         cost_estimate=pl.CostEstimate(flops=40_000_000, bytes_accessed=11_000_000, transcendentals=0),
-    )(block_columns, keys, anchor_hour, trip_counts, dest_hour, daily_target)
+    )(*[pltpu.with_memory_space_constraint(a, pltpu.HBM) for a in (block_columns, anchor_hour, trip_counts, dest_hour, daily_target)])
     return fitted, gap
 
 

time: 116 us -> 107 us (0.922)
  local copies, waits for them, and re-layouts: 9 us -> 2.79 us
  Pallas kernels: 105 us -> 103 us
  other arithmetic: 1.4 us -> 0 us
    unnamed x12 -> x2, local copies, waits for them, and re-layouts: 8.91 us -> 2.79 us
    pallas_call x1, Pallas kernels: 105 us -> 103 us  [on_device(): pl.pallas_call(kernel, out_shape=(jax.ShapeDtypeStruct(trip_counts.shape,...]
where the time goes in v2:
time: 107 us
  Pallas kernels  103 us (96%)
  local copies, waits for them, and re-layouts  2.79 us (3%)
    pallas_call x1, Pallas kernels, on_device(): pl.pallas_call(kernel, out_shape=(jax.ShapeDtypeStruct(trip_counts.shape,...  103 us
    unnamed x2, local copies, waits for them, and re-layouts  2.79 us

profile of v2, /device:TPU:1, one launch (start us, length us, event | category | flops | bytes accessed | tf_op | source)
XLA Modules:
  0.0 106.9 jit_solution(6298128450778401515)
XLA Ops:
  0.6 103.5 %shard_map.68 = (bf16[3,12,256,256]{3,2,1,0:T(8,128)(2,1)S(1)}, f32[3,512]{1,0:T(4,128)S(1)}) custom-call(s32[12]{0:T(128)} %cols_ref.1, f32[3,256]{1,0:T(4,128)} %anchor_ref.1, bf16[3,12,256,256]{3,2,1,0:T(8,128)(2,1)} %trips_ref.1, f32[3,32768]{1,0:T(4,128)} %dest_ref.1, bf16[12,256,256]{2,1,0:T(8,128)(2,1)} %target_ref.1), custom_call_target="tpu_custom_call" | custom-call | flops 40000000 | bytes 11000000 | tf_op jit(solution)/shard_map/pallas_call | solution.py:329
  104.1 2.2 %copy.9 = bf16[3,12,256,256]{3,2,1,0:T(8,128)(2,1)} copy(bf16[3,12,256,256]{3,2,1,0:T(8,128)(2,1)S(1)} %get-tuple-element.4) | data formatting | bytes 9437184
  106.3 0.6 copy.10

commit v3 on v2

--- a/solution.py
+++ b/solution.py
@@ -9,13 +9,22 @@
 SLOTS = 12
 SIDE = 256
 LANES = 128
-GROUP = 8
-DEPTH = 8
-PIECE = DEPTH * BINS * 2
+CHIPS_Z, CHIPS_Y = 8, 4
+CHIPS = CHIPS_Z * CHIPS_Y
+OWN = 8
 KEYS = 128
 ROWS = 64
 LAG = 2
 F32 = jnp.float32
+
+
+def hops(offset):
+    return min(offset[0], CHIPS_Z - offset[0]) + min(offset[1], CHIPS_Y - offset[1])
+
+
+OFFSETS = sorted(
+    [(a, b) for a in range(CHIPS_Z) for b in range(CHIPS_Y) if (a, b) != (0, 0)], key=hops, reverse=True
+)
 
 
 def send(src, dst, send_sem, recv_sem, tm, orig):
@@ -33,24 +42,25 @@
     cols_ref, anchor_ref, trips_ref, dest_ref, target_ref,
     fitted_ref, gap_ref,
     trips, part, factor, half_in, quarter_in, target, row_acc, anchor_fit, dest_row, dest8,
-    onehot, sums, spread, gains, wide, wide_in, narrow, narrow_in, gain_z, gain_piece,
+    onehot, sums, spread, gains, wide, wide_in, narrow, narrow_in,
     wide2, wide2_in, narrow2, narrow2_in,
     trips_sem, target_sem, dest_sem, fitted_sem,
     half_s, half_r, quarter_s, quarter_r, back_s, back_r, whole_s, whole_r,
-    wide_s, wide_r, narrow_s, narrow_r, gz_s, gz_r, gg_s, gg_r, wide2_s, wide2_r, narrow2_s, narrow2_r,
+    wide_sem, narrow_s, narrow_r, gain_sem, gain_s, gain_r, wide2_sem, narrow2_s, narrow2_r,
 ):
     x = lax.axis_index("tm")
     q = lax.axis_index("orig")
-    z, g = q // GROUP, q % GROUP
+    chip, core = q // 2, q % 2
+    z, y = chip // CHIPS_Y, chip % CHIPS_Y
     v = x // 2
     u = (x + v) % 2
     pa = x + 1 - 2 * (x % 2)
     pb = 3 - x
-    group = [z * GROUP + (g + d) % GROUP for d in range(1, GROUP)]
-    column = [((z + d) % DEPTH) * GROUP + g for d in range(1, DEPTH)]
+    other = chip * 2 + 1 - core
+    chips = [((z + a) % CHIPS_Z) * CHIPS_Y + (y + b) % CHIPS_Y for a, b in OFFSETS]
 
     barrier = pltpu.get_barrier_semaphore()
-    partners = [(x, o) for o in group + column] + [(pa, q), (pb, q)]
+    partners = [(x, 2 * o + core) for o in chips] + [(x, other), (pa, q), (pb, q)]
     for t_, o_ in partners:
         pl.semaphore_signal(barrier, inc=1, device_id=(t_, o_), device_id_type=pl.DeviceIdType.MESH)
 
@@ -81,27 +91,22 @@
     for h in range(2):
         load_target(h).start()
 
-    r = lax.broadcasted_iota(jnp.int32, (GROUP * PIECE, KEYS), 0)
-    rg = (r * 1366) >> 16
-    rem = r - rg * 48
-    rz = (rem * 10923) >> 16
-    rem = rem - rz * 6
-    row_key = (16 * rz + 2 * rg + (rem & 1)) * BINS + (rem >> 1)
+    r = lax.broadcasted_iota(jnp.int32, (2 * CHIPS * OWN, KEYS), 0)
+    block = 4 * ((r >> 3) & (CHIPS - 1)) + 2 * (r >> 8) + (r & 1)
+    row_key = jnp.where((r & 7) < 2 * BINS, block * BINS + ((r & 7) >> 1), -2)
     lane = lax.broadcasted_iota(jnp.int32, (1, KEYS), 1)
     key = jnp.full((1, KEYS), -1, jnp.int32)
     for s in range(SLOTS):
         col = cols_ref[s]
         in_slot = (lane >= 8 * s) & (lane < 8 * s + BINS) & (jnp.full((1, KEYS), col, jnp.int32) >= 0)
         key = jnp.where(in_slot, col * BINS + lane - 8 * s, key)
-    onehot[...] = jnp.where(row_key == key, 1.0, 0.0).astype(F32)
+    onehot[...] = jnp.where(row_key == key, 1.0, 0.0).astype(F32).reshape(2, CHIPS * OWN, KEYS)
 
     diagonal = lax.broadcasted_iota(jnp.int32, (SIDE, SIDE), 0) == lax.broadcasted_iota(
         jnp.int32, (SIDE, SIDE), 1
     )
     row_acc[...] = jnp.zeros_like(row_acc)
     sums[...] = jnp.zeros_like(sums)
-    narrow[...] = jnp.zeros_like(narrow)
-    narrow2[...] = jnp.zeros_like(narrow2)
     dest8[...] = jnp.ones_like(dest8)
 
     @pl.loop(0, SLOTS)
@@ -133,64 +138,54 @@
 
     pl.semaphore_wait(barrier, len(partners))
 
-    def owner_sums(wide, wide_in, narrow, narrow_in, wide_s, wide_r, narrow_s, narrow_r):
-        wide[...] = jnp.dot(
-            onehot[...], sums[...].reshape(KEYS, SIDE), precision=lax.Precision.HIGHEST, preferred_element_type=F32
-        )
-        copies = []
-        for d in range(1, GROUP):
-            other = pl.multiple_of(((g + d) % GROUP) * PIECE, PIECE)
-            copies.append(
-                send(wide.at[pl.ds(other, PIECE), :], wide_in.at[d - 1], wide_s.at[d - 1], wide_r.at[d - 1], x, group[d - 1])
-            )
+    def owner_sums(wide, wide_in, narrow, narrow_in, wide_sem, narrow_s, narrow_r):
+        def by_owner(c):
+            return jnp.dot(
+                onehot[c], sums[...].reshape(KEYS, SIDE), precision=lax.Precision.HIGHEST, preferred_element_type=F32
+            ).reshape(CHIPS, OWN, SIDE)
+
+        wide[...] = by_owner(1 - core)
+        copies = [send(wide, wide_in, wide_sem.at[0], wide_sem.at[1], x, other)]
+        copies[0].start()
+        kept = by_owner(core)
+        copies[0].wait_recv()
+        narrow[...] = kept + wide_in[...]
+        for i, o in enumerate(chips):
+            copies.append(send(narrow.at[o], narrow_in.at[i], narrow_s.at[i], narrow_r.at[i], x, 2 * o + core))
             copies[-1].start()
-        total = wide[pl.ds(pl.multiple_of(g * PIECE, PIECE), PIECE), :]
-        for d in range(1, GROUP):
-            copies[d - 1].wait_recv()
-            total = total + wide_in[d - 1]
-        for c in range(DEPTH):
-            narrow[c, pl.ds(0, 6), :] = total[6 * c : 6 * c + 6, :]
-        more = []
-        for d in range(1, DEPTH):
-            more.append(
-                send(narrow.at[(z + d) % DEPTH], narrow_in.at[d - 1], narrow_s.at[d - 1], narrow_r.at[d - 1], x, column[d - 1])
-            )
-            more[-1].start()
-        total = narrow[z]
-        for d in range(1, DEPTH):
-            more[d - 1].wait_recv()
-            total = total + narrow_in[d - 1]
-        return total, copies + more
+        total = narrow[chip]
+        for i in reversed(range(len(chips))):
+            copies[1 + i].wait_recv()
+            total = total + narrow_in[i]
+        return total, copies
 
     load_dest.wait()
     for t in range(BINS):
         for b in range(2):
             dest8[pl.ds(2 * t + b, 1), :] = dest_row[pl.ds(t, 1), pl.ds(b * SIDE, SIDE)]
 
-    total, pending = owner_sums(wide, wide_in, narrow, narrow_in, wide_s, wide_r, narrow_s, narrow_r)
-    gain_z[z] = dest8[...] / jnp.maximum(total, 1.0)
+    total, pending = owner_sums(wide, wide_in, narrow, narrow_in, wide_sem, narrow_s, narrow_r)
+    gains[core, chip] = dest8[...] / jnp.maximum(total, 1.0)
     copies = []
-    for d in range(1, DEPTH):
-        copies.append(send(gain_z.at[z], gain_z.at[z], gz_s.at[d - 1], gz_r.at[d - 1], x, column[d - 1]))
+    for i, o in enumerate(chips):
+        mine = gains.at[core, chip]
+        copies.append(send(mine, mine, gain_s.at[i], gain_r.at[i], x, 2 * o + core))
         copies[-1].start()
     for copy in copies:
         copy.wait_recv()
-    pending += copies
-    for c in range(DEPTH):
-        gain_piece[pl.ds(6 * c, 6), :] = gain_z[c, pl.ds(0, 6), :]
-    mine = pl.ds(pl.multiple_of(g * PIECE, PIECE), PIECE)
-    copies = []
-    for d in range(1, GROUP):
-        copies.append(send(gain_piece, gains.at[mine, :], gg_s.at[d - 1], gg_r.at[d - 1], x, group[d - 1]))
-        copies[-1].start()
-    gains[mine, :] = gain_piece[...]
-    for copy in copies:
-        copy.wait_recv()
-    pending += copies
-    spread[...] = lax.dot_general(
-        onehot[...], gains[...], (((0,), (0,)), ((), ())),
-        precision=lax.Precision.HIGHEST, preferred_element_type=F32,
-    ).reshape(KEYS // 8, 8, SIDE)
+    swap = send(gains.at[core], gains.at[core], gain_sem.at[0], gain_sem.at[1], x, other)
+    swap.start()
+
+    def by_slot(c):
+        return lax.dot_general(
+            onehot[c], gains[c].reshape(CHIPS * OWN, SIDE), (((0,), (0,)), ((), ())),
+            precision=lax.Precision.HIGHEST, preferred_element_type=F32,
+        ).reshape(KEYS // 8, 8, SIDE)
+
+    near = by_slot(core)
+    swap.wait_recv()
+    spread[...] = near + by_slot(1 - core)
+    pending += copies + [swap]
     for h in range(2):
         load_target(h).wait()
 
@@ -276,7 +271,7 @@
                     sums[s, pl.ds(t, 1), lanes] = jnp.sum(acc, axis=0, keepdims=True) * gain
             store_fitted(s).start()
 
-    total, more = owner_sums(wide2, wide2_in, narrow2, narrow2_in, wide2_s, wide2_r, narrow2_s, narrow2_r)
+    total, more = owner_sums(wide2, wide2_in, narrow2, narrow2_in, wide2_sem, narrow2_s, narrow2_r)
     pending += more
     gap = total / dest8[...] - 1.0
     for t in range(BINS):
@@ -310,22 +305,13 @@
         vmem(BINS, SIDE, LANES),
         vmem(BINS, 512),
         vmem(8, SIDE),
-        vmem(GROUP * PIECE, KEYS),
+        vmem(2, CHIPS * OWN, KEYS),
         vmem(KEYS // 8, 8, SIDE),
         vmem(KEYS // 8, 8, SIDE),
-        vmem(GROUP * PIECE, SIDE),
-        vmem(GROUP * PIECE, SIDE),
-        vmem(GROUP - 1, PIECE, SIDE),
-        vmem(DEPTH, 8, SIDE),
-        vmem(DEPTH - 1, 8, SIDE),
-        vmem(DEPTH, 8, SIDE),
-        vmem(PIECE, SIDE),
-        vmem(GROUP * PIECE, SIDE),
-        vmem(GROUP - 1, PIECE, SIDE),
-        vmem(DEPTH, 8, SIDE),
-        vmem(DEPTH - 1, 8, SIDE),
+        vmem(2, CHIPS, OWN, SIDE),
+    ] + [vmem(CHIPS, OWN, SIDE), vmem(CHIPS, OWN, SIDE), vmem(CHIPS, OWN, SIDE), vmem(CHIPS - 1, OWN, SIDE)] * 2 + [
         dma(SLOTS), dma(2), pltpu.SemaphoreType.DMA, dma(SLOTS),
-    ] + [dma(SLOTS, 2)] * 8 + [dma(7)] * 12
+    ] + [dma(SLOTS, 2)] * 8 + [dma(2), dma(CHIPS - 1), dma(CHIPS - 1)] * 3
     fitted, gap = pl.pallas_call(
         kernel,
         out_shape=(

time: 107 us -> 105 us (0.981)
  Pallas kernels: 103 us -> 101 us
    pallas_call x1, Pallas kernels: 103 us -> 101 us  [on_device(): pl.pallas_call(kernel, out_shape=(jax.ShapeDtypeStruct(trip_counts.shape,...]
where the time goes in v3:
time: 105 us; the launch traced here: 104 us
  Pallas kernels  101 us (96%)
  local copies, waits for them, and re-layouts  2.79 us (3%)
    pallas_call x1, Pallas kernels, on_device(): pl.pallas_call(kernel, out_shape=(jax.ShapeDtypeStruct(trip_counts.shape,...  101 us
    unnamed x2, local copies, waits for them, and re-layouts  2.79 us

profile of v3, /device:TPU:1, one launch (start us, length us, event | category | flops | bytes accessed | tf_op | source)
XLA Modules:
  0.0 104.5 jit_solution(6227362404260724419)
XLA Ops:
  0.6 101.0 %shard_map.68 = (bf16[3,12,256,256]{3,2,1,0:T(8,128)(2,1)S(1)}, f32[3,512]{1,0:T(4,128)S(1)}) custom-call(s32[12]{0:T(128)} %cols_ref.1, f32[3,256]{1,0:T(4,128)} %anchor_ref.1, bf16[3,12,256,256]{3,2,1,0:T(8,128)(2,1)} %trips_ref.1, f32[3,32768]{1,0:T(4,128)} %dest_ref.1, bf16[12,256,256]{2,1,0:T(8,128)(2,1)} %target_ref.1), custom_call_target="tpu_custom_call" | custom-call | flops 40000000 | bytes 11000000 | tf_op jit(solution)/shard_map/pallas_call | solution.py:315
  101.7 2.2 %copy.9 = bf16[3,12,256,256]{3,2,1,0:T(8,128)(2,1)} copy(bf16[3,12,256,256]{3,2,1,0:T(8,128)(2,1)S(1)} %get-tuple-element.4) | data formatting | bytes 9437184
  103.9 0.6 copy.10

commit v4 on v3

--- a/solution.py
+++ b/solution.py
@@ -14,6 +14,7 @@
 OWN = 8
 KEYS = 128
 ROWS = 64
+EARLY = 4
 LAG = 2
 F32 = jnp.float32
 
@@ -43,10 +44,11 @@
     fitted_ref, gap_ref,
     trips, part, factor, half_in, quarter_in, target, row_acc, anchor_fit, dest_row, dest8,
     onehot, sums, spread, gains, wide, wide_in, narrow, narrow_in,
-    wide2, wide2_in, narrow2, narrow2_in,
+    wide2, wide2_in, narrow2, narrow2_in, ship, ship_in, peer,
     trips_sem, target_sem, dest_sem, fitted_sem,
     half_s, half_r, quarter_s, quarter_r, back_s, back_r, whole_s, whole_r,
     wide_sem, narrow_s, narrow_r, gain_sem, gain_s, gain_r, wide2_sem, narrow2_s, narrow2_r,
+    ship_s, ship_r, peer_s, peer_r,
 ):
     x = lax.axis_index("tm")
     q = lax.axis_index("orig")
@@ -138,7 +140,7 @@
 
     pl.semaphore_wait(barrier, len(partners))
 
-    def owner_sums(wide, wide_in, narrow, narrow_in, wide_sem, narrow_s, narrow_r):
+    def owner_sums(wide, wide_in, narrow, narrow_in, wide_sem, narrow_s, narrow_r, meanwhile):
         def by_owner(c):
             return jnp.dot(
                 onehot[c], sums[...].reshape(KEYS, SIDE), precision=lax.Precision.HIGHEST, preferred_element_type=F32
@@ -153,18 +155,33 @@
         for i, o in enumerate(chips):
             copies.append(send(narrow.at[o], narrow_in.at[i], narrow_s.at[i], narrow_r.at[i], x, 2 * o + core))
             copies[-1].start()
+        meanwhile()
         total = narrow[chip]
         for i in reversed(range(len(chips))):
             copies[1 + i].wait_recv()
             total = total + narrow_in[i]
         return total, copies
 
+    def shipped(s, h):
+        return send(ship.at[s, h], ship_in.at[s, h], ship_s.at[s, h], ship_r.at[s, h], first[h], q)
+
+    def ship_early():
+        @pl.loop(0, EARLY)
+        def _(s):
+            for h in range(2):
+                rows = pl.ds(sent64[h], 64)
+                for t in range(BINS):
+                    for l in range(SIDE // LANES):
+                        lanes = pl.ds(l * LANES, LANES)
+                        ship[s, h, t, :, lanes] = trips[s, t, rows, lanes].astype(F32) * anchor_fit[t, rows, :]
+                shipped(s, h).start()
+
     load_dest.wait()
     for t in range(BINS):
         for b in range(2):
             dest8[pl.ds(2 * t + b, 1), :] = dest_row[pl.ds(t, 1), pl.ds(b * SIDE, SIDE)]
 
-    total, pending = owner_sums(wide, wide_in, narrow, narrow_in, wide_sem, narrow_s, narrow_r)
+    total, pending = owner_sums(wide, wide_in, narrow, narrow_in, wide_sem, narrow_s, narrow_r, ship_early)
     gains[core, chip] = dest8[...] / jnp.maximum(total, 1.0)
     copies = []
     for i, o in enumerate(chips):
@@ -186,6 +203,13 @@
     swap.wait_recv()
     spread[...] = near + by_slot(1 - core)
     pending += copies + [swap]
+    early_slots = pl.ds(0, EARLY)
+    swaps = [
+        send(spread.at[early_slots], peer.at[h], peer_s.at[h], peer_r.at[h], first[h], q) for h in range(2)
+    ]
+    for copy in swaps:
+        copy.start()
+    pending += swaps
     for h in range(2):
         load_target(h).wait()
 
@@ -212,9 +236,9 @@
 
     @pl.loop(0, SLOTS + 4 * LAG)
     def _(k):
-        @pl.when(k < SLOTS)
-        def _():
-            s = k
+        @pl.when(k < SLOTS - EARLY)
+        def _():
+            s = k + EARLY
             for l in range(SIDE // LANES):
                 lanes = pl.ds(l * LANES, LANES)
                 gain = [spread[s, pl.ds(t, 1), lanes] for t in range(BINS)]
@@ -227,9 +251,30 @@
             for h in range(2):
                 halves(s, h).start()
 
-        @pl.when((k >= LAG) & (k < SLOTS + LAG))
-        def _():
-            s = k - LAG
+        @pl.when(k == SLOTS - EARLY + LAG)
+        def _():
+            for copy in swaps:
+                copy.wait_recv()
+
+        @pl.when((k >= SLOTS - EARLY + LAG) & (k < SLOTS + LAG))
+        def _():
+            s = k - LAG - (SLOTS - EARLY)
+            for h in range(2):
+                shipped(s, h).wait_recv()
+                rows = pl.ds(kept64[h], 64)
+                for l in range(SIDE // LANES):
+                    lanes = pl.ds(l * LANES, LANES)
+                    acc = jnp.zeros((64, LANES), F32)
+                    for t in range(BINS):
+                        fit = trips[s, t, rows, lanes].astype(F32) * anchor_fit[t, rows, :]
+                        acc += fit * spread[s, pl.ds(t, 1), lanes]
+                        acc += ship_in[s, h, t, :, lanes] * peer[h, s, pl.ds(t, 1), lanes]
+                    part[s, rows, lanes] = acc
+                quarters(s, h).start()
+
+        @pl.when((k >= LAG) & (k < SLOTS - EARLY + LAG))
+        def _():
+            s = k - LAG + EARLY
             for h in range(2):
                 halves(s, h).wait_recv()
                 part[s, pl.ds(kept64[h], 64), :] += half_in[s, h]
@@ -237,7 +282,7 @@
 
         @pl.when((k >= 2 * LAG) & (k < SLOTS + 2 * LAG))
         def _():
-            s = k - 2 * LAG
+            s = lax.rem(k - 2 * LAG + EARLY, SLOTS)
             dead = jnp.where(cols_ref[s] >= 0, 0.0, 1.0).astype(F32)
             for h in range(2):
                 quarters(s, h).wait_recv()
@@ -248,14 +293,14 @@
 
         @pl.when((k >= 3 * LAG) & (k < SLOTS + 3 * LAG))
         def _():
-            s = k - 3 * LAG
+            s = lax.rem(k - 3 * LAG + EARLY, SLOTS)
             for h in range(2):
                 back(s, h).wait_recv()
                 whole(s, h).start()
 
         @pl.when(k >= 4 * LAG)
         def _():
-            s = k - 4 * LAG
+            s = lax.rem(k - 4 * LAG + EARLY, SLOTS)
             for h in range(2):
                 whole(s, h).wait_recv()
             for t in range(BINS):
@@ -271,7 +316,7 @@
                     sums[s, pl.ds(t, 1), lanes] = jnp.sum(acc, axis=0, keepdims=True) * gain
             store_fitted(s).start()
 
-    total, more = owner_sums(wide2, wide2_in, narrow2, narrow2_in, wide2_sem, narrow2_s, narrow2_r)
+    total, more = owner_sums(wide2, wide2_in, narrow2, narrow2_in, wide2_sem, narrow2_s, narrow2_r, lambda: None)
     pending += more
     gap = total / dest8[...] - 1.0
     for t in range(BINS):
@@ -281,10 +326,19 @@
     for copy in pending:
         copy.wait_send()
 
-    @pl.loop(0, SLOTS)
+    @pl.loop(0, EARLY)
+    def _(s):
+        for h in range(2):
+            shipped(s, h).wait_send()
+
+    @pl.loop(EARLY, SLOTS)
     def _(s):
         for h in range(2):
             halves(s, h).wait_send()
+
+    @pl.loop(0, SLOTS)
+    def _(s):
+        for h in range(2):
             quarters(s, h).wait_send()
             back(s, h).wait_send()
             whole(s, h).wait_send()
@@ -310,8 +364,11 @@
         vmem(KEYS // 8, 8, SIDE),
         vmem(2, CHIPS, OWN, SIDE),
     ] + [vmem(CHIPS, OWN, SIDE), vmem(CHIPS, OWN, SIDE), vmem(CHIPS, OWN, SIDE), vmem(CHIPS - 1, OWN, SIDE)] * 2 + [
+        vmem(EARLY, 2, BINS, 64, SIDE),
+        vmem(EARLY, 2, BINS, 64, SIDE),
+        vmem(2, EARLY, 8, SIDE),
         dma(SLOTS), dma(2), pltpu.SemaphoreType.DMA, dma(SLOTS),
-    ] + [dma(SLOTS, 2)] * 8 + [dma(2), dma(CHIPS - 1), dma(CHIPS - 1)] * 3
+    ] + [dma(SLOTS, 2)] * 8 + [dma(2), dma(CHIPS - 1), dma(CHIPS - 1)] * 3 + [dma(EARLY, 2)] * 2 + [dma(2)] * 2
     fitted, gap = pl.pallas_call(
         kernel,
         out_shape=(

time: 105 us -> 100 us (0.952)
  Pallas kernels: 101 us -> 96.5 us
    pallas_call x1, Pallas kernels: 101 us -> 96.5 us  [on_device(): pl.pallas_call(kernel, out_shape=(jax.ShapeDtypeStruct(trip_counts.shape,...]
where the time goes in v4:
time: 100 us
  Pallas kernels  96.5 us (96%)
  local copies, waits for them, and re-layouts  2.79 us (3%)
    pallas_call x1, Pallas kernels, on_device(): pl.pallas_call(kernel, out_shape=(jax.ShapeDtypeStruct(trip_counts.shape,...  96.5 us
    unnamed x2, local copies, waits for them, and re-layouts  2.79 us

profile of v4, /device:TPU:1, one launch (start us, length us, event | category | flops | bytes accessed | tf_op | source)
XLA Modules:
  0.0 100.0 jit_solution(11591429087266688210)
XLA Ops:
  0.6 96.5 %shard_map.68 = (bf16[3,12,256,256]{3,2,1,0:T(8,128)(2,1)S(1)}, f32[3,512]{1,0:T(4,128)S(1)}) custom-call(s32[12]{0:T(128)} %cols_ref.1, f32[3,256]{1,0:T(4,128)} %anchor_ref.1, bf16[3,12,256,256]{3,2,1,0:T(8,128)(2,1)} %trips_ref.1, f32[3,32768]{1,0:T(4,128)} %dest_ref.1, bf16[12,256,256]{2,1,0:T(8,128)(2,1)} %target_ref.1), custom_call_target="tpu_custom_call" | custom-call | flops 40000000 | bytes 11000000 | tf_op jit(solution)/shard_map/pallas_call | solution.py:372
  97.2 2.2 %copy.9 = bf16[3,12,256,256]{3,2,1,0:T(8,128)(2,1)} copy(bf16[3,12,256,256]{3,2,1,0:T(8,128)(2,1)S(1)} %get-tuple-element.4) | data formatting | bytes 9437184
  99.4 0.6 copy.10

commit v5 on v4

--- a/solution.py
+++ b/solution.py
@@ -12,11 +12,22 @@
 CHIPS_Z, CHIPS_Y = 8, 4
 CHIPS = CHIPS_Z * CHIPS_Y
 OWN = 8
+USED = 2 * BINS
 KEYS = 128
 ROWS = 64
 EARLY = 4
+AT_ONCE = 1
 LAG = 2
 F32 = jnp.float32
+BF16 = jnp.bfloat16
+
+
+def picked(onehot, values):
+    high = values.astype(BF16)
+    rest = values - high.astype(F32)
+    middle = rest.astype(BF16)
+    low = (rest - middle.astype(F32)).astype(BF16)
+    return sum(jnp.dot(onehot, part, preferred_element_type=F32) for part in (low, middle, high))
 
 
 def hops(offset):
@@ -43,7 +54,7 @@
     cols_ref, anchor_ref, trips_ref, dest_ref, target_ref,
     fitted_ref, gap_ref,
     trips, part, factor, half_in, quarter_in, target, row_acc, anchor_fit, dest_row, dest8,
-    onehot, sums, spread, gains, wide, wide_in, narrow, narrow_in,
+    onehot, by_key, sums, spread, gains, wide, wide_in, narrow, narrow_in,
     wide2, wide2_in, narrow2, narrow2_in, ship, ship_in, peer,
     trips_sem, target_sem, dest_sem, fitted_sem,
     half_s, half_r, quarter_s, quarter_r, back_s, back_r, whole_s, whole_r,
@@ -102,13 +113,18 @@
         col = cols_ref[s]
         in_slot = (lane >= 8 * s) & (lane < 8 * s + BINS) & (jnp.full((1, KEYS), col, jnp.int32) >= 0)
         key = jnp.where(in_slot, col * BINS + lane - 8 * s, key)
-    onehot[...] = jnp.where(row_key == key, 1.0, 0.0).astype(F32).reshape(2, CHIPS * OWN, KEYS)
+    match = jnp.where(row_key == key, 1.0, 0.0).astype(F32)
+    for c in range(2):
+        half = match[c * CHIPS * OWN : (c + 1) * CHIPS * OWN, :]
+        onehot[c] = half.astype(BF16)
+        by_key[c] = half.T.astype(BF16)
 
     diagonal = lax.broadcasted_iota(jnp.int32, (SIDE, SIDE), 0) == lax.broadcasted_iota(
         jnp.int32, (SIDE, SIDE), 1
     )
     row_acc[...] = jnp.zeros_like(row_acc)
     sums[...] = jnp.zeros_like(sums)
+    gains[...] = jnp.zeros_like(gains)
     dest8[...] = jnp.ones_like(dest8)
 
     @pl.loop(0, SLOTS)
@@ -138,13 +154,36 @@
                     acc += trips[s, t, rows, lanes].astype(F32) * anchor_fit[t, rows, :]
                 sums[s, pl.ds(t, 1), lanes] = jnp.sum(acc, axis=0, keepdims=True)
 
+    def shipped(s, h):
+        return send(ship.at[s, h], ship_in.at[s, h], ship_s.at[s, h], ship_r.at[s, h], first[h], q)
+
+    def fill_early(s):
+        for h in range(2):
+            rows = pl.ds(sent64[h], 64)
+            for t in range(BINS):
+                for l in range(SIDE // LANES):
+                    lanes = pl.ds(l * LANES, LANES)
+                    ship[s, h, t, :, lanes] = trips[s, t, rows, lanes].astype(F32) * anchor_fit[t, rows, :]
+
+    def send_early(s):
+        for h in range(2):
+            shipped(s, h).start()
+
+    def later_early():
+        @pl.loop(AT_ONCE, EARLY)
+        def _(s):
+            fill_early(s)
+            send_early(s)
+
+    pl.loop(0, AT_ONCE)(fill_early)
     pl.semaphore_wait(barrier, len(partners))
+    pl.loop(0, AT_ONCE)(send_early)
+
+    used = pl.ds(0, USED)
 
     def owner_sums(wide, wide_in, narrow, narrow_in, wide_sem, narrow_s, narrow_r, meanwhile):
         def by_owner(c):
-            return jnp.dot(
-                onehot[c], sums[...].reshape(KEYS, SIDE), precision=lax.Precision.HIGHEST, preferred_element_type=F32
-            ).reshape(CHIPS, OWN, SIDE)
+            return picked(onehot[c], sums[...].reshape(KEYS, SIDE)).reshape(CHIPS, OWN, SIDE)
 
         wide[...] = by_owner(1 - core)
         copies = [send(wide, wide_in, wide_sem.at[0], wide_sem.at[1], x, other)]
@@ -153,39 +192,25 @@
         copies[0].wait_recv()
         narrow[...] = kept + wide_in[...]
         for i, o in enumerate(chips):
-            copies.append(send(narrow.at[o], narrow_in.at[i], narrow_s.at[i], narrow_r.at[i], x, 2 * o + core))
+            copies.append(send(narrow.at[o, used, :], narrow_in.at[i, used, :], narrow_s.at[i], narrow_r.at[i], x, 2 * o + core))
             copies[-1].start()
         meanwhile()
-        total = narrow[chip]
+        total = narrow[chip, used, :]
         for i in reversed(range(len(chips))):
             copies[1 + i].wait_recv()
-            total = total + narrow_in[i]
+            total = total + narrow_in[i, used, :]
         return total, copies
-
-    def shipped(s, h):
-        return send(ship.at[s, h], ship_in.at[s, h], ship_s.at[s, h], ship_r.at[s, h], first[h], q)
-
-    def ship_early():
-        @pl.loop(0, EARLY)
-        def _(s):
-            for h in range(2):
-                rows = pl.ds(sent64[h], 64)
-                for t in range(BINS):
-                    for l in range(SIDE // LANES):
-                        lanes = pl.ds(l * LANES, LANES)
-                        ship[s, h, t, :, lanes] = trips[s, t, rows, lanes].astype(F32) * anchor_fit[t, rows, :]
-                shipped(s, h).start()
 
     load_dest.wait()
     for t in range(BINS):
         for b in range(2):
             dest8[pl.ds(2 * t + b, 1), :] = dest_row[pl.ds(t, 1), pl.ds(b * SIDE, SIDE)]
 
-    total, pending = owner_sums(wide, wide_in, narrow, narrow_in, wide_sem, narrow_s, narrow_r, ship_early)
-    gains[core, chip] = dest8[...] / jnp.maximum(total, 1.0)
+    total, pending = owner_sums(wide, wide_in, narrow, narrow_in, wide_sem, narrow_s, narrow_r, later_early)
+    gains[core, chip, used, :] = dest8[used, :] / jnp.maximum(total, 1.0)
     copies = []
     for i, o in enumerate(chips):
-        mine = gains.at[core, chip]
+        mine = gains.at[core, chip, used, :]
         copies.append(send(mine, mine, gain_s.at[i], gain_r.at[i], x, 2 * o + core))
         copies[-1].start()
     for copy in copies:
@@ -194,10 +219,7 @@
     swap.start()
 
     def by_slot(c):
-        return lax.dot_general(
-            onehot[c], gains[c].reshape(CHIPS * OWN, SIDE), (((0,), (0,)), ((), ())),
-            precision=lax.Precision.HIGHEST, preferred_element_type=F32,
-        ).reshape(KEYS // 8, 8, SIDE)
+        return picked(by_key[c], gains[c].reshape(CHIPS * OWN, SIDE)).reshape(KEYS // 8, 8, SIDE)
 
     near = by_slot(core)
     swap.wait_recv()
@@ -318,7 +340,7 @@
 
     total, more = owner_sums(wide2, wide2_in, narrow2, narrow2_in, wide2_sem, narrow2_s, narrow2_r, lambda: None)
     pending += more
-    gap = total / dest8[...] - 1.0
+    gap = total / dest8[used, :] - 1.0
     for t in range(BINS):
         for b in range(2):
             gap_ref[pl.ds(t, 1), pl.ds(b * SIDE, SIDE)] = gap[2 * t + b : 2 * t + b + 1, :]
@@ -359,7 +381,8 @@
         vmem(BINS, SIDE, LANES),
         vmem(BINS, 512),
         vmem(8, SIDE),
-        vmem(2, CHIPS * OWN, KEYS),
+        pltpu.VMEM((2, CHIPS * OWN, KEYS), BF16),
+        pltpu.VMEM((2, KEYS, CHIPS * OWN), BF16),
         vmem(KEYS // 8, 8, SIDE),
         vmem(KEYS // 8, 8, SIDE),
         vmem(2, CHIPS, OWN, SIDE),

time: 100 us -> 95.7 us (0.957)
  Pallas kernels: 96.5 us -> 92.2 us
    pallas_call x1, Pallas kernels: 96.5 us -> 92.2 us  [on_device(): pl.pallas_call(kernel, out_shape=(jax.ShapeDtypeStruct(trip_counts.shape,...]
where the time goes in v5:
time: 95.7 us; the launch traced here: 95.6 us
  Pallas kernels  92.2 us (96%)
  local copies, waits for them, and re-layouts  2.79 us (3%)
    pallas_call x1, Pallas kernels, on_device(): pl.pallas_call(kernel, out_shape=(jax.ShapeDtypeStruct(trip_counts.shape,...  92.2 us
    unnamed x2, local copies, waits for them, and re-layouts  2.79 us

profile of v5, /device:TPU:1, one launch (start us, length us, event | category | flops | bytes accessed | tf_op | source)
XLA Modules:
  0.0 95.6 jit_solution(9435276503082274957)
XLA Ops:
  0.6 92.2 %shard_map.68 = (bf16[3,12,256,256]{3,2,1,0:T(8,128)(2,1)S(1)}, f32[3,512]{1,0:T(4,128)S(1)}) custom-call(s32[12]{0:T(128)} %cols_ref.1, f32[3,256]{1,0:T(4,128)} %anchor_ref.1, bf16[3,12,256,256]{3,2,1,0:T(8,128)(2,1)} %trips_ref.1, f32[3,32768]{1,0:T(4,128)} %dest_ref.1, bf16[12,256,256]{2,1,0:T(8,128)(2,1)} %target_ref.1), custom_call_target="tpu_custom_call" | custom-call | flops 40000000 | bytes 11000000 | tf_op jit(solution)/shard_map/pallas_call | solution.py:395
  92.8 2.2 %copy.9 = bf16[3,12,256,256]{3,2,1,0:T(8,128)(2,1)} copy(bf16[3,12,256,256]{3,2,1,0:T(8,128)(2,1)S(1)} %get-tuple-element.4) | data formatting | bytes 9437184
  95.0 0.6 copy.10

commit v6 on v5

--- a/solution.py
+++ b/solution.py
@@ -16,6 +16,7 @@
 KEYS = 128
 ROWS = 64
 EARLY = 4
+FIRST = 4
 AT_ONCE = 1
 LAG = 2
 F32 = jnp.float32
@@ -55,11 +56,11 @@
     fitted_ref, gap_ref,
     trips, part, factor, half_in, quarter_in, target, row_acc, anchor_fit, dest_row, dest8,
     onehot, by_key, sums, spread, gains, wide, wide_in, narrow, narrow_in,
-    wide2, wide2_in, narrow2, narrow2_in, ship, ship_in, peer,
+    wide2, wide2_in, narrow2, narrow2_in, ship, ship_in, peer, col_out, col_in,
     trips_sem, target_sem, dest_sem, fitted_sem,
     half_s, half_r, quarter_s, quarter_r, back_s, back_r, whole_s, whole_r,
     wide_sem, narrow_s, narrow_r, gain_sem, gain_s, gain_r, wide2_sem, narrow2_s, narrow2_r,
-    ship_s, ship_r, peer_s, peer_r,
+    ship_s, ship_r, peer_s, peer_r, col_s, col_r,
 ):
     x = lax.axis_index("tm")
     q = lax.axis_index("orig")
@@ -253,14 +254,51 @@
         rows = pl.ds(kept64[h], 64)
         return send(factor.at[s, rows, :], factor.at[s, rows, :], whole_s.at[s, h], whole_r.at[s, h], first[h], q)
 
+    def columns(s, h):
+        rows = pl.ds(0, BINS)
+        return send(
+            col_out.at[s, h, rows, :], col_in.at[s, h, rows, :], col_s.at[s, h], col_r.at[s, h], first[h], q
+        )
+
     def store_fitted(s):
         return pltpu.make_async_copy(trips.at[s], fitted_ref.at[:, s], fitted_sem.at[s])
 
+    def finish(s, with_sums):
+        for h in range(2):
+            whole(s, h).wait_recv()
+        for t in range(BINS):
+            for l in range(SIDE // LANES):
+                lanes = pl.ds(l * LANES, LANES)
+                gain = spread[s, pl.ds(t, 1), lanes]
+                acc = jnp.zeros((ROWS, LANES), F32)
+                for c in range(SIDE // ROWS):
+                    rows = pl.ds(c * ROWS, ROWS)
+                    value = trips[s, t, rows, lanes].astype(F32) * anchor_fit[t, rows, :] * factor[s, rows, lanes]
+                    acc += value
+                    trips[s, t, rows, lanes] = (value * gain).astype(jnp.bfloat16)
+                if with_sums:
+                    sums[s, pl.ds(t, 1), lanes] = jnp.sum(acc, axis=0, keepdims=True) * gain
+        store_fitted(s).start()
+
+    def finish_early():
+        @pl.loop(0, EARLY)
+        def _(s):
+            finish(s, False)
+
+    def early_at(p):
+        return (p >= FIRST) & (p < FIRST + EARLY)
+
+    def later_at(p):
+        return ((p >= 0) & (p < FIRST)) | ((p >= FIRST + EARLY) & (p < SLOTS))
+
+    def slot_at(p):
+        return jnp.where(p < FIRST, p + EARLY, jnp.where(p < FIRST + EARLY, p - FIRST, p))
+
     @pl.loop(0, SLOTS + 4 * LAG)
     def _(k):
-        @pl.when(k < SLOTS - EARLY)
-        def _():
-            s = k + EARLY
+        @pl.when(later_at(k))
+        def _():
+            s = slot_at(k)
             for l in range(SIDE // LANES):
                 lanes = pl.ds(l * LANES, LANES)
                 gain = [spread[s, pl.ds(t, 1), lanes] for t in range(BINS)]
@@ -273,14 +311,14 @@
             for h in range(2):
                 halves(s, h).start()
 
-        @pl.when(k == SLOTS - EARLY + LAG)
+        @pl.when(k == FIRST + LAG)
         def _():
             for copy in swaps:
                 copy.wait_recv()
 
-        @pl.when((k >= SLOTS - EARLY + LAG) & (k < SLOTS + LAG))
-        def _():
-            s = k - LAG - (SLOTS - EARLY)
+        @pl.when(early_at(k - LAG))
+        def _():
+            s = slot_at(k - LAG)
             for h in range(2):
                 shipped(s, h).wait_recv()
                 rows = pl.ds(kept64[h], 64)
@@ -294,9 +332,9 @@
                     part[s, rows, lanes] = acc
                 quarters(s, h).start()
 
-        @pl.when((k >= LAG) & (k < SLOTS - EARLY + LAG))
-        def _():
-            s = k - LAG + EARLY
+        @pl.when(later_at(k - LAG))
+        def _():
+            s = slot_at(k - LAG)
             for h in range(2):
                 halves(s, h).wait_recv()
                 part[s, pl.ds(kept64[h], 64), :] += half_in[s, h]
@@ -304,7 +342,7 @@
 
         @pl.when((k >= 2 * LAG) & (k < SLOTS + 2 * LAG))
         def _():
-            s = lax.rem(k - 2 * LAG + EARLY, SLOTS)
+            s = slot_at(k - 2 * LAG)
             dead = jnp.where(cols_ref[s] >= 0, 0.0, 1.0).astype(F32)
             for h in range(2):
                 quarters(s, h).wait_recv()
@@ -313,32 +351,51 @@
                 factor[s, rows, :] = target[h, s].astype(F32) / (daily + dead)
                 back(s, h).start()
 
-        @pl.when((k >= 3 * LAG) & (k < SLOTS + 3 * LAG))
-        def _():
-            s = lax.rem(k - 3 * LAG + EARLY, SLOTS)
+        @pl.when(later_at(k - 3 * LAG))
+        def _():
+            s = slot_at(k - 3 * LAG)
             for h in range(2):
                 back(s, h).wait_recv()
                 whole(s, h).start()
 
-        @pl.when(k >= 4 * LAG)
-        def _():
-            s = lax.rem(k - 4 * LAG + EARLY, SLOTS)
-            for h in range(2):
-                whole(s, h).wait_recv()
+        @pl.when(early_at(k - 3 * LAG))
+        def _():
+            s = slot_at(k - 3 * LAG)
+            for h in range(2):
+                back(s, h).wait_recv()
             for t in range(BINS):
                 for l in range(SIDE // LANES):
                     lanes = pl.ds(l * LANES, LANES)
-                    gain = spread[s, pl.ds(t, 1), lanes]
-                    acc = jnp.zeros((ROWS, LANES), F32)
-                    for c in range(SIDE // ROWS):
-                        rows = pl.ds(c * ROWS, ROWS)
-                        value = trips[s, t, rows, lanes].astype(F32) * anchor_fit[t, rows, :] * factor[s, rows, lanes]
-                        acc += value
-                        trips[s, t, rows, lanes] = (value * gain).astype(jnp.bfloat16)
-                    sums[s, pl.ds(t, 1), lanes] = jnp.sum(acc, axis=0, keepdims=True) * gain
-            store_fitted(s).start()
-
-    total, more = owner_sums(wide2, wide2_in, narrow2, narrow2_in, wide2_sem, narrow2_s, narrow2_r, lambda: None)
+                    own = jnp.zeros((64, LANES), F32)
+                    for h in range(2):
+                        rows = pl.ds(kept64[h], 64)
+                        ratio = factor[s, rows, lanes]
+                        own += trips[s, t, rows, lanes].astype(F32) * anchor_fit[t, rows, :] * ratio
+                        total = jnp.sum(ship_in[s, h, t, :, lanes] * ratio, axis=0, keepdims=True)
+                        col_out[s, h, pl.ds(t, 1), lanes] = total * peer[h, s, pl.ds(t, 1), lanes]
+                    total = jnp.sum(own, axis=0, keepdims=True)
+                    sums[s, pl.ds(t, 1), lanes] = total * spread[s, pl.ds(t, 1), lanes]
+            for h in range(2):
+                columns(s, h).start()
+
+        @pl.when(later_at(k - 4 * LAG))
+        def _():
+            finish(slot_at(k - 4 * LAG), True)
+
+        @pl.when(early_at(k - 4 * LAG))
+        def _():
+            s = slot_at(k - 4 * LAG)
+            rows = pl.ds(0, BINS)
+            for h in range(2):
+                columns(s, h).wait_recv()
+                sums[s, rows, :] += col_in[s, h, rows, :]
+
+    @pl.loop(0, EARLY)
+    def _(s):
+        for h in range(2):
+            whole(s, h).start()
+
+    total, more = owner_sums(wide2, wide2_in, narrow2, narrow2_in, wide2_sem, narrow2_s, narrow2_r, finish_early)
     pending += more
     gap = total / dest8[used, :] - 1.0
     for t in range(BINS):
@@ -352,6 +409,7 @@
     def _(s):
         for h in range(2):
             shipped(s, h).wait_send()
+            columns(s, h).wait_send()
 
     @pl.loop(EARLY, SLOTS)
     def _(s):
@@ -390,8 +448,10 @@
         vmem(EARLY, 2, BINS, 64, SIDE),
         vmem(EARLY, 2, BINS, 64, SIDE),
         vmem(2, EARLY, 8, SIDE),
+        vmem(EARLY, 2, 8, SIDE),
+        vmem(EARLY, 2, 8, SIDE),
         dma(SLOTS), dma(2), pltpu.SemaphoreType.DMA, dma(SLOTS),
-    ] + [dma(SLOTS, 2)] * 8 + [dma(2), dma(CHIPS - 1), dma(CHIPS - 1)] * 3 + [dma(EARLY, 2)] * 2 + [dma(2)] * 2
+    ] + [dma(SLOTS, 2)] * 8 + [dma(2), dma(CHIPS - 1), dma(CHIPS - 1)] * 3 + [dma(EARLY, 2)] * 2 + [dma(2)] * 2 + [dma(EARLY, 2)] * 2
     fitted, gap = pl.pallas_call(
         kernel,
         out_shape=(

time: 95.7 us -> 91.9 us (0.960)
  Pallas kernels: 92.2 us -> 88.4 us
    pallas_call x1, Pallas kernels: 92.2 us -> 88.4 us  [on_device(): pl.pallas_call(kernel, out_shape=(jax.ShapeDtypeStruct(trip_counts.shape,...]
where the time goes in v6:
time: 91.9 us; the launch traced here: 91.8 us
  Pallas kernels  88.4 us (96%)
  local copies, waits for them, and re-layouts  2.79 us (3%)
    pallas_call x1, Pallas kernels, on_device(): pl.pallas_call(kernel, out_shape=(jax.ShapeDtypeStruct(trip_counts.shape,...  88.4 us
    unnamed x2, local copies, waits for them, and re-layouts  2.79 us

profile of v6, /device:TPU:1, one launch (start us, length us, event | category | flops | bytes accessed | tf_op | source)
XLA Modules:
  0.0 91.8 jit_solution(6629838562786847142)
XLA Ops:
  0.6 88.4 %shard_map.68 = (bf16[3,12,256,256]{3,2,1,0:T(8,128)(2,1)S(1)}, f32[3,512]{1,0:T(4,128)S(1)}) custom-call(s32[12]{0:T(128)} %cols_ref.1, f32[3,256]{1,0:T(4,128)} %anchor_ref.1, bf16[3,12,256,256]{3,2,1,0:T(8,128)(2,1)} %trips_ref.1, f32[3,32768]{1,0:T(4,128)} %dest_ref.1, bf16[12,256,256]{2,1,0:T(8,128)(2,1)} %target_ref.1), custom_call_target="tpu_custom_call" | custom-call | flops 40000000 | bytes 11000000 | tf_op jit(solution)/shard_map/pallas_call | solution.py:455
  89.0 2.2 %copy.9 = bf16[3,12,256,256]{3,2,1,0:T(8,128)(2,1)} copy(bf16[3,12,256,256]{3,2,1,0:T(8,128)(2,1)S(1)} %get-tuple-element.4) | data formatting | bytes 9437184
  91.2 0.6 copy.10

commit v7 on v6

--- a/solution.py
+++ b/solution.py
@@ -18,7 +18,7 @@
 EARLY = 4
 FIRST = 4
 AT_ONCE = 1
-LAG = 2
+LAG = 3
 F32 = jnp.float32
 BF16 = jnp.bfloat16
 
@@ -177,21 +177,22 @@
             send_early(s)
 
     pl.loop(0, AT_ONCE)(fill_early)
+    def by_owner(c):
+        return picked(onehot[c], sums[...].reshape(KEYS, SIDE)).reshape(CHIPS, OWN, SIDE)
+
+    wide[...] = by_owner(1 - core)
+    narrow[...] = by_owner(core)
     pl.semaphore_wait(barrier, len(partners))
     pl.loop(0, AT_ONCE)(send_early)
 
     used = pl.ds(0, USED)
 
-    def owner_sums(wide, wide_in, narrow, narrow_in, wide_sem, narrow_s, narrow_r, meanwhile):
-        def by_owner(c):
-            return picked(onehot[c], sums[...].reshape(KEYS, SIDE)).reshape(CHIPS, OWN, SIDE)
-
-        wide[...] = by_owner(1 - core)
+    def owner_sums(wide, wide_in, narrow, narrow_in, wide_sem, narrow_s, narrow_r, beside, meanwhile):
         copies = [send(wide, wide_in, wide_sem.at[0], wide_sem.at[1], x, other)]
         copies[0].start()
-        kept = by_owner(core)
+        beside()
         copies[0].wait_recv()
-        narrow[...] = kept + wide_in[...]
+        narrow[...] += wide_in[...]
         for i, o in enumerate(chips):
             copies.append(send(narrow.at[o, used, :], narrow_in.at[i, used, :], narrow_s.at[i], narrow_r.at[i], x, 2 * o + core))
             copies[-1].start()
@@ -207,7 +208,7 @@
         for b in range(2):
             dest8[pl.ds(2 * t + b, 1), :] = dest_row[pl.ds(t, 1), pl.ds(b * SIDE, SIDE)]
 
-    total, pending = owner_sums(wide, wide_in, narrow, narrow_in, wide_sem, narrow_s, narrow_r, later_early)
+    total, pending = owner_sums(wide, wide_in, narrow, narrow_in, wide_sem, narrow_s, narrow_r, lambda: None, later_early)
     gains[core, chip, used, :] = dest8[used, :] / jnp.maximum(total, 1.0)
     copies = []
     for i, o in enumerate(chips):
@@ -395,7 +396,12 @@
         for h in range(2):
             whole(s, h).start()
 
-    total, more = owner_sums(wide2, wide2_in, narrow2, narrow2_in, wide2_sem, narrow2_s, narrow2_r, finish_early)
+    wide2[...] = by_owner(1 - core)
+
+    def near_product():
+        narrow2[...] = by_owner(core)
+
+    total, more = owner_sums(wide2, wide2_in, narrow2, narrow2_in, wide2_sem, narrow2_s, narrow2_r, near_product, finish_early)
     pending += more
     gap = total / dest8[used, :] - 1.0
     for t in range(BINS):

time: 91.9 us -> 91.5 us (level)
  no operation moved by 1% of the time
where the time goes in v7:
time: 91.5 us; the launch traced here: 91.4 us
  Pallas kernels  88 us (96%)
  local copies, waits for them, and re-layouts  2.79 us (3%)
    pallas_call x1, Pallas kernels, on_device(): pl.pallas_call(kernel, out_shape=(jax.ShapeDtypeStruct(trip_counts.shape,...  88 us
    unnamed x2, local copies, waits for them, and re-layouts  2.79 us

profile of v7, /device:TPU:1, one launch (start us, length us, event | category | flops | bytes accessed | tf_op | source)
XLA Modules:
  0.0 91.4 jit_solution(17426731808692724506)
XLA Ops:
  0.6 88.0 %shard_map.68 = (bf16[3,12,256,256]{3,2,1,0:T(8,128)(2,1)S(1)}, f32[3,512]{1,0:T(4,128)S(1)}) custom-call(s32[12]{0:T(128)} %cols_ref.1, f32[3,256]{1,0:T(4,128)} %anchor_ref.1, bf16[3,12,256,256]{3,2,1,0:T(8,128)(2,1)} %trips_ref.1, f32[3,32768]{1,0:T(4,128)} %dest_ref.1, bf16[12,256,256]{2,1,0:T(8,128)(2,1)} %target_ref.1), custom_call_target="tpu_custom_call" | custom-call | flops 40000000 | bytes 11000000 | tf_op jit(solution)/shard_map/pallas_call | solution.py:461
  88.6 2.2 %copy.9 = bf16[3,12,256,256]{3,2,1,0:T(8,128)(2,1)} copy(bf16[3,12,256,256]{3,2,1,0:T(8,128)(2,1)S(1)} %get-tuple-element.4) | data formatting | bytes 9437184
  90.8 0.6 copy.10

commit v8 on v7

--- a/solution.py
+++ b/solution.py
@@ -173,10 +173,9 @@
     def later_early():
         @pl.loop(AT_ONCE, EARLY)
         def _(s):
-            fill_early(s)
             send_early(s)
 
-    pl.loop(0, AT_ONCE)(fill_early)
+    pl.loop(0, EARLY)(fill_early)
     def by_owner(c):
         return picked(onehot[c], sums[...].reshape(KEYS, SIDE)).reshape(CHIPS, OWN, SIDE)
 

time: 91.5 us -> 91.9 us (level)
  no operation moved by 1% of the time
where the time goes in v8:
time: 91.9 us; the launch traced here: 91.8 us
  Pallas kernels  88.3 us (96%)
  local copies, waits for them, and re-layouts  2.79 us (3%)
    pallas_call x1, Pallas kernels, on_device(): pl.pallas_call(kernel, out_shape=(jax.ShapeDtypeStruct(trip_counts.shape,...  88.3 us
    unnamed x2, local copies, waits for them, and re-layouts  2.79 us

profile of v8, /device:TPU:1, one launch (start us, length us, event | category | flops | bytes accessed | tf_op | source)
XLA Modules:
  0.0 91.8 jit_solution(7923862164375196490)
XLA Ops:
  0.6 88.3 %shard_map.68 = (bf16[3,12,256,256]{3,2,1,0:T(8,128)(2,1)S(1)}, f32[3,512]{1,0:T(4,128)S(1)}) custom-call(s32[12]{0:T(128)} %cols_ref.1, f32[3,256]{1,0:T(4,128)} %anchor_ref.1, bf16[3,12,256,256]{3,2,1,0:T(8,128)(2,1)} %trips_ref.1, f32[3,32768]{1,0:T(4,128)} %dest_ref.1, bf16[12,256,256]{2,1,0:T(8,128)(2,1)} %target_ref.1), custom_call_target="tpu_custom_call" | custom-call | flops 40000000 | bytes 11000000 | tf_op jit(solution)/shard_map/pallas_call | solution.py:460
  89.0 2.2 %copy.9 = bf16[3,12,256,256]{3,2,1,0:T(8,128)(2,1)} copy(bf16[3,12,256,256]{3,2,1,0:T(8,128)(2,1)S(1)} %get-tuple-element.4) | data formatting | bytes 9437184
  91.2 0.6 copy.10
